TPU v7x, 256 devices: a whole 4x4x8 slice. The times are simulated.
256 devices in a mesh: wa: 8 (over z), vert: 32 (over y, x, core).
Axes of the slice: x: 4, y: 4, z: 8, core: 2. Of those that a mesh axis runs over, the one named last changes fastest.
Arguments:
- hidden_in: bfloat16 [384, 8192], P(None, 'wa')
- gate_levels: bfloat16 [8192, 28672], P('wa', 'vert'), may hold values from -127 to 127, as said below
- up_levels: bfloat16 [8192, 28672], P('wa', 'vert'), may hold values from -127 to 127, as said below
- gate_scale: float32 [28672], P('vert'), as said below
- up_scale: float32 [28672], P('vert'), as said below
- down_levels: bfloat16 [28672, 8192], P('vert', 'wa'), may hold values from -127 to 127, as said below
- down_scale: float32 [8192], P('wa'), as said below
- norm_gain: float32 [8192], P('wa'), may hold values from 0.5 to 1.5
- head_weight: bfloat16 [8192, 16000], P('wa', 'vert')
- reward_states: bfloat16 [8, 384, 4096], P('wa', None, 'vert'), may hold values from -6 to 6
- reward_gain: float32 [8, 4096], P('wa'), may hold values from 0.5 to 1.5
- reward_heads: bfloat16 [8, 4096, 16000], P('wa', None, 'vert')
- preference: int32 [384, 8], P(None, 'wa'), may hold values from 0 to 16
- token_ids: int32 [384], P('wa'), may hold values from 0 to 15999
Outputs:
- log_probs: float32 [384, 16000], P('wa', 'vert')
- chosen: float32 [384], P('wa')
Inputs may be any that keep to these rules, and one draw needn't show every extreme that they name: `gate_levels`: whole numbers. `up_levels`: whole numbers. `down_levels`: whole numbers. `gate_scale`: positive. `up_scale`: positive. `down_scale`: positive.
All inputs are finite; a program needn't handle non-finite values.
Results may differ from a plain program's by a relative error of at most 0.0025.
Values may be sent and summed in bfloat16 or wider, within the bound.
No kernel may reach another device: no remote copies, remote signals or barrier semaphores. Data moves between devices by JAX's collectives and lax.ppermute only.
A program may use at most 64 MiB of HBM per device.

v0:
```python
import jax
import jax.numpy as jnp
from jax import lax
from jax.sharding import PartitionSpec as P

D = 8192


def log_total(values):
    local_top = jnp.max(values, axis=-1)
    top = lax.pmax(local_top, "vert")
    total = lax.psum(jnp.sum(jnp.exp(values - top[..., None]), axis=-1), "vert")
    return top + jnp.log(total)


def normalize(resid, norm_gain):
    squares = lax.psum(jnp.sum(resid * resid, axis=1), "wa")
    return (resid * lax.rsqrt(squares[:, None] / D + 1e-05) * norm_gain).astype(jnp.bfloat16)


def local(
    hidden_in,
    gate_levels,
    up_levels,
    gate_scale,
    up_scale,
    down_levels,
    down_scale,
    norm_gain,
    head_weight,
    reward_states,
    reward_gain,
    reward_heads,
    preference,
    token_ids,
):
    gate_part = jnp.dot(hidden_in, gate_levels, preferred_element_type=jnp.float32)
    up_part = jnp.dot(hidden_in, up_levels, preferred_element_type=jnp.float32)
    gate, up = lax.psum((gate_part, up_part), "wa")
    hidden = (jax.nn.silu(gate * gate_scale) * (up * up_scale)).astype(jnp.bfloat16)
    down_part = jnp.dot(hidden, down_levels, preferred_element_type=jnp.float32)
    down = lax.psum(down_part, "vert") * down_scale
    resid = hidden_in.astype(jnp.float32) + down
    normed = normalize(resid, norm_gain)
    base_part = jnp.dot(normed, head_weight, preferred_element_type=jnp.float32)
    states = lax.all_gather(reward_states, "vert", axis=2, tiled=True)
    state_values = states.astype(jnp.float32)
    state_scale = lax.rsqrt(jnp.mean(state_values * state_values, axis=2, keepdims=True) + 1e-05)
    reward_normed = (state_values * state_scale * reward_gain[:, None, :]).astype(jnp.bfloat16)
    reward_logits = jnp.einsum(
        "rnd,rdv->rnv", reward_normed, reward_heads, preferred_element_type=jnp.float32
    )
    reward_logp = reward_logits - log_total(reward_logits)[..., None]
    weights = preference.astype(jnp.float32).T / 16.0
    weighted = jnp.sum(weights[:, :, None] * reward_logp, axis=0)
    base_rows, reward_rows = (
        lax.psum_scatter(base_part, "wa", scatter_dimension=0, tiled=True),
        lax.psum_scatter(weighted, "wa", scatter_dimension=0, tiled=True),
    )
    base_logp = base_rows - log_total(base_rows)[:, None]
    mix = base_logp + reward_rows
    log_probs = mix - log_total(mix)[:, None]
    columns = log_probs.shape[1]
    vocab_index = lax.axis_index("vert") * columns + lax.iota(jnp.int32, columns)
    picked = jnp.sum(jnp.where(vocab_index[None, :] == token_ids[:, None], log_probs, 0.0), axis=1)
    chosen = lax.psum(picked, "vert")
    return (log_probs, chosen)


def solution(mesh):
    return jax.shard_map(
        local,
        mesh=mesh,
        in_specs=(
            P(None, "wa"),
            P("wa", "vert"),
            P("wa", "vert"),
            P("vert"),
            P("vert"),
            P("vert", "wa"),
            P("wa"),
            P("wa"),
            P("wa", "vert"),
            P("wa", None, "vert"),
            P("wa", None),
            P("wa", None, "vert"),
            P(None, "wa"),
            P("wa"),
        ),
        out_specs=(P("wa", "vert"), P("wa")),
        check_vma=False,
    )
```

profile of v0, /device:TPU:1, one launch (start us, length us, event | category | flops | bytes accessed | tf_op | source)
XLA Modules:
  0.0 702.5 jit_solution(15787238454085852242)
XLA Ops:
  7.2 3.9 fusion.17
  11.2 2.0 fusion.18
  13.3 89.1 %all-reduce.8.cloned.1.call-done = (f32[384,896]{1,0:T(8,128)}, f32[384,896]{1,0:T(8,128)}) async-done(((f32[384,896]{1,0:T(8,128)}, f32[384,896]{1,0:T(8,128)}), (f32[384,896]{1,0:T(8,128)}, f32[384,896]{1,0:T(8,128)})) %all-reduce.8.cloned.1.call-update) | async-done | bytes 2752528 | tf_op jit(solution)/shard_map/psum | solution.py:39
  102.5 3.9 fusion.13
  106.5 0.0 reduce-scatter.7.cloned.1.call-start
  106.5 116.9 %all-reduce.6.cloned.1.call-done = f32[384,1024]{1,0:T(8,128)} async-done(((f32[384,1024]{1,0:T(8,128)}), f32[384,1024]{1,0:T(8,128)}) %all-reduce.6.cloned.1.call-update) | async-done | bytes 1572880 | tf_op jit(solution)/shard_map/psum | solution.py:42
  223.4 2.1 multiply_reduce_fusion
  225.4 13.7 %psum.59 = f32[384]{0:T(512)S(1)} all-reduce(f32[384]{0:T(512)S(1)} %multiply_reduce_fusion), channel_id=1, replica_groups=mesh['wa'=8,'vert'=32] {'wa'}, use_global_device_ids=true, to_apply=%region_4.5 | all-reduce | flops 384 | bytes 3072 | tf_op jit(solution)/shard_map/psum | solution.py:17
  239.1 3.0 fusion.9
  242.2 0.5 all-gather.2.cloned.1.call-update
  242.8 33.5 %reduce-scatter.7.cloned.1.call-done = f32[48,500]{1,0:T(8,128)} async-done(((f32[384,500]{1,0:T(8,128)}), f32[48,500]{1,0:T(8,128)}) %reduce-scatter.7.cloned.1.call-update) | async-done | bytes 96016
  276.3 1.0 copy.23
  277.4 1.1 reduce_max.29
  278.5 55.9 %all-gather.2.cloned.1.call-done = bf16[1,384,4096]{2,1,0:T(8,128)(2,1)} async-done(((bf16[1,384,128]{2,1,0:T(8,128)(2,1)}), bf16[1,384,4096]{2,1,0:T(8,128)(2,1)}) %all-gather.2.cloned.1.call-update) | async-done | bytes 3145744 | tf_op jit(solution)/shard_map/all_gather | solution.py:46
  334.3 2.7 fusion
  337.1 0.1 copy-done.2
  337.2 4.6 fusion.16
  341.8 62.3 %all-reduce.1 = (f32[1,384]{1,0:T(1,128)S(1)}, f32[48]{0:T(128)S(1)}) all-reduce(f32[1,384]{1,0:T(1,128)S(1)} %reduce_max.31, f32[48]{0:T(128)S(1)} %reduce_max.29), channel_id=1, replica_groups=mesh['wa'=8,'vert'=32] {'vert'}, use_global_device_ids=true, to_apply=%region_12.13 | all-reduce | flops 432 | bytes 3456 | tf_op jit(solution)/shard_map/pmax | solution.py:11
  404.1 0.2 exponential_reduce_fusion
  404.3 0.1 exponential_reduce_fusion.2
  404.4 65.2 %all-reduce = (f32[1,384]{1,0:T(1,128)S(1)}, f32[48]{0:T(128)S(1)}) all-reduce(f32[1,384]{1,0:T(1,128)S(1)} %reduce_sum.64, f32[48]{0:T(128)S(1)} %exponential_reduce_fusion.2), channel_id=1, replica_groups=mesh['wa'=8,'vert'=32] {'vert'}, use_global_device_ids=true, to_apply=%region_14.15 | all-reduce | flops 432 | bytes 3456 | tf_op jit(solution)/shard_map/psum | solution.py:12
  469.6 0.1 subtract_multiply_fusion
  469.7 1.2 copy.24
  471.0 29.6 %reduce-scatter.9.cloned.1.call-done = f32[48,500]{1,0:T(8,128)} async-done(((f32[384,500]{1,0:T(8,128)}), f32[48,500]{1,0:T(8,128)}) %reduce-scatter.9.cloned.1.call-update) | async-done | bytes 96016
  500.5 1.0 copy.25
  501.6 0.1 fusion.15
  501.7 67.5 %pmax.23 = f32[48]{0:T(128)S(1)} all-reduce(f32[48]{0:T(128)S(1)} %get-tuple-element.14), channel_id=1, replica_groups=mesh['wa'=8,'vert'=32] {'vert'}, use_global_device_ids=true, to_apply=%region_17.18 | all-reduce | flops 48 | bytes 384 | tf_op jit(solution)/shard_map/pmax | solution.py:11
  569.2 0.1 exponential_reduce_fusion.1
  569.3 62.7 %psum.62 = f32[48]{0:T(128)S(1)} all-reduce(f32[48]{0:T(128)S(1)} %exponential_reduce_fusion.1), channel_id=1, replica_groups=mesh['wa'=8,'vert'=32] {'vert'}, use_global_device_ids=true, to_apply=%region_19.20 | all-reduce | flops 48 | bytes 384 | tf_op jit(solution)/shard_map/psum | solution.py:12
  632.0 0.2 select_reduce_fusion
  632.1 0.8 copy.20
  632.9 63.2 %psum.63 = f32[48]{0:T(128)} all-reduce(f32[48]{0:T(128)S(1)} %get-tuple-element.12), channel_id=1, replica_groups=mesh['wa'=8,'vert'=32] {'vert'}, use_global_device_ids=true, to_apply=%region_21.22 | all-reduce | flops 48 | bytes 384 | tf_op jit(solution)/shard_map/psum | solution.py:66
  (45 shorter events, 0.4 us)
Async XLA Ops:
  7.2 95.3 %copy-start = (bf16[896,1024]{1,0:T(8,128)(2,1)S(1)}, bf16[896,1024]{1,0:T(8,128)(2,1)}, u32[]{:S(2)}) copy-start(bf16[896,1024]{1,0:T(8,128)(2,1)} %param.19) | copy-start | bytes 5505028
  7.2 4.0 copy-start.3
  7.2 95.3 %all-reduce.8.cloned.1.call-start = ((), (), s32[]{:S(2)}) async-start(), calls=%async_computation.6 | async-start | bytes 5505024 | tf_op jit(solution)/shard_map/psum | solution.py:39
  7.2 4.0 copy-start.10
  13.2 89.2 %copy-start.12 = (f32[896]{0:T(1024)S(1)}, f32[896]{0:T(1024)}, u32[]{:S(2)}) copy-start(f32[896]{0:T(1024)} %param.18) | copy-start | bytes 10756
  13.2 89.2 %copy-start.13 = (f32[896]{0:T(1024)S(1)}, f32[896]{0:T(1024)}, u32[]{:S(2)}) copy-start(f32[896]{0:T(1024)} %param.17) | copy-start | bytes 10756
  13.3 210.1 %all-reduce.6.cloned.1.call-start = ((), (), s32[]{:S(2)}) async-start(), calls=%async_computation.2 | async-start | bytes 3145728 | tf_op jit(solution)/shard_map/psum | solution.py:42
  106.4 116.9 %copy-start.6 = (f32[1024]{0:T(1024)S(1)}, f32[1024]{0:T(1024)}, u32[]{:S(2)}) copy-start(f32[1024]{0:T(1024)} %param.20) | copy-start | bytes 12292
  106.4 132.7 %copy-start.7 = (f32[1024]{0:T(1024)S(1)}, f32[1024]{0:T(1024)}, u32[]{:S(2)}) copy-start(f32[1024]{0:T(1024)} %param.21) | copy-start | bytes 12292
  106.5 169.9 %reduce-scatter.7.cloned.1.call-start = ((), (), s32[]{:S(2)}) async-start(), calls=%async_computation.4 | async-start | bytes 884736
  223.4 15.8 %copy-start.1 = (f32[384,1024]{1,0:T(8,128)S(1)}, f32[384,1024]{1,0:T(8,128)}, u32[]{:S(2)}) copy-start(f32[384,1024]{1,0:T(8,128)} %all-reduce.6.cloned.1.call-done) | copy-start | bytes 4718596
  239.1 3.6 copy-start.8
  242.1 92.2 %all-gather.2.cloned.1.call-start = ((), (), s32[]{:S(2)}) async-start(), calls=%async_computation.3 | async-start | bytes 3244032 | tf_op jit(solution)/shard_map/all_gather | solution.py:46
  242.7 257.8 %reduce-scatter.9.cloned.1.call-start = ((), (), s32[]{:S(2)}) async-start(), calls=%async_computation.5 | async-start | bytes 884736
  277.3 126.9 %copy-start.4 = (f32[48,500]{0,1:T(8,128)}, f32[48,500]{0,1:T(8,128)S(1)}, u32[]{:S(2)}) copy-start(f32[48,500]{0,1:T(8,128)S(1)} %copy.23) | copy-start | bytes 288004
  277.4 59.7 %copy-start.11 = (f32[1,4096]{1,0:T(1,128)S(1)}, f32[1,4096]{1,0:T(1,128)}, u32[]{:S(2)}) copy-start(f32[1,4096]{1,0:T(1,128)} %param.24) | copy-start | bytes 49156
  334.3 2.8 copy-start.2
  469.7 31.8 %copy-start.5 = (f32[48,500]{0,1:T(8,128)S(1)}, f32[48,500]{0,1:T(8,128)}, u32[]{:S(2)}) copy-start(f32[48,500]{0,1:T(8,128)} %copy-done.4) | copy-start | bytes 288004
  469.7 162.2 %copy-start.9 = (s32[48]{0:T(128)S(1)}, s32[48]{0:T(128)}, u32[]{:S(2)}) copy-start(s32[48]{0:T(128)} %param.27) | copy-start | bytes 580
Sparse Core Ops, SparseCore 0:
  13.4 89.0 all-reduce.7
  106.6 116.7 all-reduce.5
  242.3 34.0 reduce-scatter.6
  279.0 55.3 all-gather.1
  471.1 29.4 reduce-scatter.8
where the time goes:
time: 703 us
  blocking collectives  335 us (48%)
  waiting for transfers between devices  326 us (46%)
  matrix products  17.5 us (2%)
  between operations  13.9 us (2%)
    pmax x2, blocking collectives, log_total(): top = lax.pmax(local_top, 'vert')  130 us
    psum x2, blocking collectives, log_total(): total = lax.psum(jnp.sum(jnp.exp(values - top[..., None]), axis=-1), 'vert')  128 us
    psum x1, waiting for transfers between devices, local(): down = lax.psum(down_part, 'vert') * down_scale  117 us
    psum x1, waiting for transfers between devices, local(): gate, up = lax.psum((gate_part, up_part), 'wa')  89.1 us
    unnamed x7, waiting for transfers between devices  63.7 us
    psum x1, blocking collectives, local(): chosen = lax.psum(picked, 'vert')  63.2 us
    all_gather x1, waiting for transfers between devices, local(): states = lax.all_gather(reward_states, 'vert', axis=2, tiled=True)  55.9 us
  transfers between devices with their start and end apart: 5, of which 5 were waited for; matrix products, arithmetic and copies ran while one was open for 0% of the time, Pallas kernels for 0%

commit v1 on v0

--- a/solution.py
+++ b/solution.py
@@ -43,7 +43,9 @@
     resid = hidden_in.astype(jnp.float32) + down
     normed = normalize(resid, norm_gain)
     base_part = jnp.dot(normed, head_weight, preferred_element_type=jnp.float32)
-    states = lax.all_gather(reward_states, "vert", axis=2, tiled=True)
+    states = jnp.concatenate(
+        lax.all_to_all(jnp.stack([reward_states] * lax.axis_size("vert")), "vert", 0, 0), axis=2
+    )
     state_values = states.astype(jnp.float32)
     state_scale = lax.rsqrt(jnp.mean(state_values * state_values, axis=2, keepdims=True) + 1e-05)
     reward_normed = (state_values * state_scale * reward_gain[:, None, :]).astype(jnp.bfloat16)

time: 703 us -> 639 us (0.909)
  waiting for transfers between devices: 326 us -> 247 us
  starting transfers between devices: 0.2 us -> 8.93 us
    all_gather x1 -> x0, waiting for transfers between devices: 55.9 us -> none  [local(): states = lax.all_gather(reward_states, 'vert', axis=2, tiled=True)]
    psum x1, waiting for transfers between devices: 89.1 us -> 77.2 us  [local(): gate, up = lax.psum((gate_part, up_part), 'wa')]
    unnamed x7 -> x6, waiting for transfers between devices: 63.7 us -> 52.4 us
    all_to_all x0 -> x1, starting transfers between devices: none -> 8.77 us  [local(): lax.all_to_all(jnp.stack([reward_states] * lax.axis_size('vert')), 'vert'...]
  transfers between devices with their start and end apart: 5 -> 5, of which waited for: 5 -> 4; matrix products, arithmetic and copies ran while one was open for 0% -> 3% of each run, Pallas kernels for 0% -> 0%
where the time goes in v1:
time: 639 us
  blocking collectives  337 us (53%)
  waiting for transfers between devices  247 us (39%)
  matrix products  15.3 us (2%)
  between operations  14 us (2%)
  other arithmetic  8.99 us (1%)
  starting transfers between devices  8.93 us (1%)
  local copies, waits for them, and re-layouts  7.82 us (1%)
    pmax x2, blocking collectives, log_total(): top = lax.pmax(local_top, 'vert')  135 us
    psum x2, blocking collectives, log_total(): total = lax.psum(jnp.sum(jnp.exp(values - top[..., None]), axis=-1), 'vert')  125 us
    psum x1, waiting for transfers between devices, local(): down = lax.psum(down_part, 'vert') * down_scale  117 us
    psum x1, waiting for transfers between devices, local(): gate, up = lax.psum((gate_part, up_part), 'wa')  77.2 us
    psum x1, blocking collectives, local(): chosen = lax.psum(picked, 'vert')  63.2 us
    unnamed x6, waiting for transfers between devices  52.4 us
    psum x1, blocking collectives, normalize(): squares = lax.psum(jnp.sum(resid * resid, axis=1), 'wa')  13.7 us
  transfers between devices with their start and end apart: 5, of which 4 were waited for; matrix products, arithmetic and copies ran while one was open for 3% of the time, Pallas kernels for 0%

profile of v1, /device:TPU:1, one launch (start us, length us, event | category | flops | bytes accessed | tf_op | source)
XLA Modules:
  0.0 638.8 jit_solution(884959455518435105)
XLA Ops:
  7.2 4.0 fusion.14
  11.2 2.1 fusion.13
  13.3 0.9 copy-done.5
  14.2 0.1 copy.27
  14.3 2.2 stack.2
  16.5 8.8 %all-to-all-start = ((bf16[32,1,384,128]{2,3,1,0:T(8,128)(2,1)}), bf16[32,1,384,128]{2,3,1,0:T(8,128)(2,1)}, u32[]{:S(2)}, u32[]{:S(2)}) async-start(bf16[32,1,384,128]{2,3,1,0:T(8,128)(2,1)} %stack.2), calls=%async_computation | async-start | bytes 6291456 | tf_op jit(solution)/shard_map/all_to_all | solution.py:47
  25.3 77.2 %all-reduce.8.cloned.1.call-done = (f32[384,896]{1,0:T(8,128)}, f32[384,896]{1,0:T(8,128)}) async-done(((f32[384,896]{1,0:T(8,128)}, f32[384,896]{1,0:T(8,128)}), (f32[384,896]{1,0:T(8,128)}, f32[384,896]{1,0:T(8,128)})) %all-reduce.8.cloned.1.call-update) | async-done | bytes 2752528 | tf_op jit(solution)/shard_map/psum | solution.py:39
  102.6 3.9 fusion.9
  106.6 116.9 %all-reduce.6.cloned.1.call-done = f32[384,1024]{1,0:T(8,128)} async-done(((f32[384,1024]{1,0:T(8,128)}), f32[384,1024]{1,0:T(8,128)}) %all-reduce.6.cloned.1.call-update) | async-done | bytes 1572880 | tf_op jit(solution)/shard_map/psum | solution.py:42
  223.5 2.1 multiply_reduce_fusion
  225.5 13.7 %psum.59 = f32[384]{0:T(512)S(1)} all-reduce(f32[384]{0:T(512)S(1)} %multiply_reduce_fusion), channel_id=1, replica_groups=mesh['wa'=8,'vert'=32] {'wa'}, use_global_device_ids=true, to_apply=%region_4.5 | all-reduce | flops 384 | bytes 3072 | tf_op jit(solution)/shard_map/psum | solution.py:17
  239.3 3.0 fusion.5
  242.4 2.7 fusion
  245.1 2.5 fusion.2
  247.6 0.6 copy-done.11
  248.2 2.3 fusion.12
  250.5 25.4 %reduce-scatter.7.cloned.1.call-done = f32[48,500]{1,0:T(8,128)} async-done(((f32[384,500]{1,0:T(8,128)}), f32[48,500]{1,0:T(8,128)}) %reduce-scatter.7.cloned.1.call-update) | async-done | bytes 96016
  275.9 1.0 reduce_max.29
  276.9 67.6 %all-reduce.1 = (f32[1,384]{1,0:T(1,128)S(1)}, f32[48]{0:T(128)S(1)}) all-reduce(f32[1,384]{1,0:T(1,128)S(1)} %reduce_max.31, f32[48]{0:T(128)S(1)} %reduce_max.29), channel_id=1, replica_groups=mesh['wa'=8,'vert'=32] {'vert'}, use_global_device_ids=true, to_apply=%region_12.13 | all-reduce | flops 432 | bytes 3456 | tf_op jit(solution)/shard_map/pmax | solution.py:11
  344.5 0.2 exponential_reduce_fusion
  344.7 1.0 copy.32
  345.8 62.7 %all-reduce = (f32[1,384]{1,0:T(1,128)S(1)}, f32[48]{0:T(128)S(1)}) all-reduce(f32[1,384]{1,0:T(1,128)S(1)} %reduce_sum.64, f32[48]{0:T(128)S(1)} %exponential_reduce_fusion.2), channel_id=1, replica_groups=mesh['wa'=8,'vert'=32] {'vert'}, use_global_device_ids=true, to_apply=%region_14.15 | all-reduce | flops 432 | bytes 3456 | tf_op jit(solution)/shard_map/psum | solution.py:12
  408.6 1.2 copy.33
  409.9 26.9 %reduce-scatter.9.cloned.1.call-done = f32[48,500]{1,0:T(8,128)} async-done(((f32[384,500]{1,0:T(8,128)}), f32[48,500]{1,0:T(8,128)}) %reduce-scatter.9.cloned.1.call-update) | async-done | bytes 96016
  436.8 1.0 copy.34
  437.8 0.1 fusion.11
  437.9 67.5 %pmax.23 = f32[48]{0:T(128)S(1)} all-reduce(f32[48]{0:T(128)S(1)} %get-tuple-element.14), channel_id=1, replica_groups=mesh['wa'=8,'vert'=32] {'vert'}, use_global_device_ids=true, to_apply=%region_17.18 | all-reduce | flops 48 | bytes 384 | tf_op jit(solution)/shard_map/pmax | solution.py:11
  505.4 0.1 exponential_reduce_fusion.1
  505.5 62.7 %psum.62 = f32[48]{0:T(128)S(1)} all-reduce(f32[48]{0:T(128)S(1)} %exponential_reduce_fusion.1), channel_id=1, replica_groups=mesh['wa'=8,'vert'=32] {'vert'}, use_global_device_ids=true, to_apply=%region_19.20 | all-reduce | flops 48 | bytes 384 | tf_op jit(solution)/shard_map/psum | solution.py:12
  568.2 0.2 select_reduce_fusion
  568.3 0.8 copy.29
  569.1 63.2 %psum.63 = f32[48]{0:T(128)} all-reduce(f32[48]{0:T(128)S(1)} %get-tuple-element.12), channel_id=1, replica_groups=mesh['wa'=8,'vert'=32] {'vert'}, use_global_device_ids=true, to_apply=%region_21.22 | all-reduce | flops 48 | bytes 384 | tf_op jit(solution)/shard_map/psum | solution.py:68
  (49 shorter events, 0.6 us)
Async XLA Ops:
  7.2 95.4 %copy-start = (bf16[896,1024]{1,0:T(8,128)(2,1)S(1)}, bf16[896,1024]{1,0:T(8,128)(2,1)}, u32[]{:S(2)}) copy-start(bf16[896,1024]{1,0:T(8,128)(2,1)} %param.19) | copy-start | bytes 5505028
  7.2 4.0 copy-start.2
  7.2 95.4 %all-reduce.8.cloned.1.call-start = ((), (), s32[]{:S(2)}) async-start(), calls=%async_computation.6 | async-start | bytes 5505024 | tf_op jit(solution)/shard_map/psum | solution.py:39
  7.2 4.0 copy-start.12
  13.3 0.9 copy-start.5
  16.5 86.1 %copy-start.13 = (f32[896]{0:T(1024)S(1)}, f32[896]{0:T(1024)}, u32[]{:S(2)}) copy-start(f32[896]{0:T(1024)} %param.18) | copy-start | bytes 10756
  16.5 86.1 %copy-start.14 = (f32[896]{0:T(1024)S(1)}, f32[896]{0:T(1024)}, u32[]{:S(2)}) copy-start(f32[896]{0:T(1024)} %param.17) | copy-start | bytes 10756
  16.5 225.9 %all-to-all-start = ((bf16[32,1,384,128]{2,3,1,0:T(8,128)(2,1)}), bf16[32,1,384,128]{2,3,1,0:T(8,128)(2,1)}, u32[]{:S(2)}, u32[]{:S(2)}) async-start(bf16[32,1,384,128]{2,3,1,0:T(8,128)(2,1)} %stack.2), calls=%async_computation | async-start | bytes 6291456 | tf_op jit(solution)/shard_map/all_to_all | solution.py:47
  25.3 198.2 %all-reduce.6.cloned.1.call-start = ((), (), s32[]{:S(2)}) async-start(), calls=%async_computation.3 | async-start | bytes 3145728 | tf_op jit(solution)/shard_map/psum | solution.py:42
  106.5 117.0 %copy-start.7 = (f32[1024]{0:T(1024)S(1)}, f32[1024]{0:T(1024)}, u32[]{:S(2)}) copy-start(f32[1024]{0:T(1024)} %param.20) | copy-start | bytes 12292
  106.5 132.7 %copy-start.8 = (f32[1024]{0:T(1024)S(1)}, f32[1024]{0:T(1024)}, u32[]{:S(2)}) copy-start(f32[1024]{0:T(1024)} %param.21) | copy-start | bytes 12292
  106.5 169.4 %reduce-scatter.7.cloned.1.call-start = ((), (), s32[]{:S(2)}) async-start(), calls=%async_computation.4 | async-start | bytes 884736
  223.5 15.8 %copy-start.1 = (f32[384,1024]{1,0:T(8,128)S(1)}, f32[384,1024]{1,0:T(8,128)}, u32[]{:S(2)}) copy-start(f32[384,1024]{1,0:T(8,128)} %all-reduce.6.cloned.1.call-done) | copy-start | bytes 4718596
  239.3 3.1 copy-start.9
  242.3 194.5 %reduce-scatter.9.cloned.1.call-start = ((), (), s32[]{:S(2)}) async-start(), calls=%async_computation.5 | async-start | bytes 884736
  242.4 2.7 copy-start.6
  245.1 3.1 copy-start.11
  345.7 62.8 %copy-start.3 = (f32[48,500]{0,1:T(8,128)}, f32[48,500]{0,1:T(8,128)S(1)}, u32[]{:S(2)}) copy-start(f32[48,500]{0,1:T(8,128)S(1)} %copy.32) | copy-start | bytes 288004
  408.6 29.2 %copy-start.4 = (f32[48,500]{0,1:T(8,128)S(1)}, f32[48,500]{0,1:T(8,128)}, u32[]{:S(2)}) copy-start(f32[48,500]{0,1:T(8,128)} %copy-done.3) | copy-start | bytes 288004
  408.6 159.6 %copy-start.10 = (s32[48]{0:T(128)S(1)}, s32[48]{0:T(128)}, u32[]{:S(2)}) copy-start(s32[48]{0:T(128)} %param.27) | copy-start | bytes 580
Sparse Core Ops, SparseCore 0:
  13.4 89.0 all-reduce.7
  106.7 116.7 all-reduce.5
  242.4 33.4 reduce-scatter.6
  409.9 26.8 reduce-scatter.8
